TPU v7x, 256 devices: a whole 4x4x8 slice. The times are simulated.
256 devices in a mesh: dp: 16 (over y, x), shard: 16 (over z, core).
Axes of the slice: x: 4, y: 4, z: 8, core: 2. Of those that a mesh axis runs over, the one named last changes fastest.
Arguments:
- grad_partial: bfloat16 [16, 16, 1024, 1024], P('dp', None, 'shard'), may hold values from -64 to 64
- owner_slots: int32 [16], replicated, may hold values from 0 to 15, each once
- left_roots: float32 [16, 1024, 1024], P('shard', None, 'dp'), may hold values from -0.2 to 1.6, as said below
- right_roots: float32 [16, 1024, 1024], P('shard', 'dp'), may hold values from -0.2 to 1.6, as said below
- momentum: float32 [16, 1024, 1024], P('shard', 'dp'), may hold values from -6 to 6
Outputs:
- direction: bfloat16 [16, 1024, 1024], P(None, ('dp', 'shard'))
- new_momentum: float32 [16, 1024, 1024], P('shard', 'dp')
Inputs may be any that keep to these rules, and one draw needn't show every extreme that they name: `owner_slots`: every slot is named once; slot p is owned by shard index p. `left_roots`: every block is symmetric. `right_roots`: every block is symmetric.
All inputs are finite; a program needn't handle non-finite values.
Results may differ from a plain program's by a relative error of at most 0.0006.
Values may be sent and summed in bfloat16 or wider, within the bound.
A program may use at most 64 MiB of HBM per device.

v0:
```python
import jax
import jax.numpy as jnp
from jax import lax
from jax.sharding import PartitionSpec as P

epsilon = 1e-06
decay_rate = 0.9


def right_fold(operand, incoming):
    return jnp.einsum(
        "brc,bcj->brj",
        operand,
        incoming,
        precision=lax.Precision.HIGHEST,
        preferred_element_type=jnp.float32,
    )


def body(grad_partial, owner_slots, left_roots, right_roots, momentum):
    shards = lax.axis_size("shard")
    groups = lax.axis_size("dp")
    local_grad = grad_partial[0]
    block_count, slab_rows, block_width = local_grad.shape
    owned_count = block_count // shards
    quarter = block_width // groups
    piece_rows = quarter // shards
    counting = jnp.arange(block_count, dtype=jnp.int32)
    inverse = jnp.zeros((block_count,), jnp.int32).at[owner_slots].set(counting)
    slot_order = inverse.reshape(shards, owned_count).T.reshape(-1)
    arranged = jnp.take(local_grad, slot_order, axis=0).reshape(
        owned_count, shards, slab_rows, block_width
    )
    routed = lax.all_to_all(arranged, "shard", split_axis=1, concat_axis=1, tiled=True)
    routed = routed.astype(jnp.float32)
    summed = lax.psum_scatter(routed, "dp", scatter_dimension=1, tiled=True).reshape(
        owned_count, quarter, block_width
    )
    grad_sq = jnp.sum(summed * summed, axis=(1, 2))
    grad_total = lax.psum(grad_sq, "dp")
    right_part = right_fold(summed, lax.all_gather(right_roots, "dp", axis=1, tiled=True))
    reduced = lax.psum_scatter(
        jnp.einsum(
            "bic,bcj->ibj",
            left_roots,
            right_part,
            precision=lax.Precision.HIGHEST,
            preferred_element_type=jnp.float32,
        ),
        "dp",
        scatter_dimension=0,
        tiled=True,
    )
    precond = jnp.transpose(reduced, (1, 0, 2))
    prec_sq = jnp.sum(precond * precond, axis=(1, 2))
    prec_total = lax.psum(prec_sq, "dp")
    entries = block_width * block_width
    graft_scale = jnp.sqrt(grad_total / entries + epsilon) / jnp.sqrt(
        prec_total / entries + epsilon
    )
    graft = precond * graft_scale[:, None, None]
    new_momentum = decay_rate * momentum + graft
    heading = (decay_rate * new_momentum + graft).astype(jnp.bfloat16)
    outgoing = heading.reshape(owned_count, shards, piece_rows, block_width)
    returned = lax.all_to_all(outgoing, "shard", split_axis=1, concat_axis=0, tiled=True)
    returned = returned.reshape(block_count, piece_rows, block_width)
    direction = jnp.take(returned, owner_slots, axis=0)
    return (direction, new_momentum)


def solution(mesh):
    return jax.shard_map(
        body,
        mesh=mesh,
        in_specs=(
            P("dp", None, "shard", None),
            P(),
            P("shard", None, "dp"),
            P("shard", "dp", None),
            P("shard", "dp", None),
        ),
        out_specs=(P(None, ("dp", "shard"), None), P("shard", "dp", None)),
        check_vma=False,
    )
```

profile of v0, /device:TPU:1, one launch (start us, length us, event | category | flops | bytes accessed | tf_op | source)
XLA Modules:
  0.0 361.3 jit_solution(1050899775173975734)
XLA Ops:
  7.2 0.0 copy-start
  7.2 0.0 all-gather.2.cloned.1.call-start
  7.2 0.7 all-gather.2.cloned.1.call-update
  7.9 0.0 reduce-scatter.7.cloned.1.call-start
  8.0 0.7 compare_select_fusion.1
  8.6 0.6 scatter_custom_fusion
  9.3 2.0 gather_fusion
  11.3 1.8 bitcast_select_fusion
  13.2 60.8 %all_to_all.14 = bf16[1,16,64,1024]{3,2,0,1:T(8,128)(2,1)S(1)} all-to-all(bf16[1,16,64,1024]{3,2,0,1:T(8,128)(2,1)S(1)} %bitcast_select_fusion), channel_id=1, replica_groups=mesh['dp'=16,'shard'=16] {'shard'}, dimensions={1} | all-to-all | bytes 4194304 | tf_op jit(solution)/shard_map/all_to_all | solution.py:34
  74.0 2.5 bitcast_convert_fusion
  76.4 0.0 reduce-scatter.7.cloned.1.call-update
  76.4 0.0 all-reduce.5.cloned.1.call-start
  76.5 0.0 all-gather.2.cloned.1.call-done
  76.5 78.7 %reduce-scatter.7.cloned.1.call-done = f32[1,1,64,1024]{3,2,1,0:T(8,128)} async-done(((f32[1,16,64,1024]{3,2,1,0:T(8,128)}), f32[1,1,64,1024]{3,2,1,0:T(8,128)}) %reduce-scatter.7.cloned.1.call-update) | async-done | bytes 262160
  155.3 4.9 %fusion = f32[64,1024]{1,0:T(8,128)S(1)} fusion(f32[1,1024,1024]{2,1,0:T(8,128)} %all-gather.2.cloned.1.call-done, f32[1,1,64,1024]{3,2,1,0:T(8,128)} %reduce-scatter.7.cloned.1.call-done), kind=kOutput, calls=%fused_computation.3 | convolution fusion | flops 805306368 | bytes 4718592 | tf_op jit(solution)/shard_map/brc,bcj->brj/dot_general | solution.py:11
  160.2 5.1 %convolution_bitcast_fusion = f32[1024,1,1024]{0,2,1:T(8,128)} fusion(f32[64,1024]{1,0:T(8,128)S(1)} %fusion, f32[1,1024,64]{1,2,0:T(8,128)S(1)} %copy-done.2), kind=kOutput, calls=%fused_computation.5 | convolution fusion | flops 805306368 | bytes 4718592 | tf_op jit(solution)/shard_map/bic,bcj->ibj/dot_general | solution.py:43
  165.3 11.0 %copy.14 = f32[1024,1,1024]{2,1,0:T(1,128)} copy(f32[1024,1,1024]{0,2,1:T(8,128)} %convolution_bitcast_fusion) | data formatting | bytes 8388608 | tf_op jit(solution)/shard_map/bic,bcj->ibj/transpose | solution.py:43
  176.3 0.0 all-reduce.5.cloned.1.call-update
  176.3 0.6 copy-done.5
  176.9 0.6 dynamic-slice
  178.2 0.7 multiply_reduce_fusion.1
  178.8 112.1 %all-reduce.5.cloned.1.call-done = f32[1024,1,1024]{2,1,0:T(1,128)} async-done(((f32[1024,1,1024]{2,1,0:T(1,128)}), f32[1024,1,1024]{2,1,0:T(1,128)}) %all-reduce.5.cloned.1.call-update) | async-done | bytes 4194320
  290.9 2.1 multiply_reduce_fusion
  293.0 32.0 %all-reduce.2 = (f32[1]{0:T(128)}, f32[1]{0:T(128)}) all-reduce(f32[1]{0:T(128)} %bitcast.8, f32[1]{0:T(128)} %bitcast.9), channel_id=1, replica_groups=mesh['dp'=16,'shard'=16] {'dp'}, use_global_device_ids=true, to_apply=%region_4.5 | all-reduce | flops 2 | bytes 16 | tf_op jit(solution)/shard_map/psum | solution.py:40
  326.4 0.0 copy-done.3
  326.4 2.1 fusion.3
  328.5 0.7 reshape.95
  329.2 14.9 %all-to-all-start.1 = ((bf16[1,16,4,1024]{3,2,0,1:T(4,128)(2,1)}), bf16[1,16,4,1024]{3,2,0,1:T(4,128)(2,1)S(1)}, u32[]{:S(2)}, u32[]{:S(2)}) async-start(bf16[1,16,4,1024]{3,2,0,1:T(4,128)(2,1)} %bitcast.12), calls=%async_computation.1 | async-start | bytes 262144 | tf_op jit(solution)/shard_map/all_to_all | solution.py:65
  344.2 0.8 copy.16
  344.9 8.4 %all-to-all-done.1 = bf16[1,16,4,1024]{3,2,0,1:T(4,128)(2,1)S(1)} async-done(((bf16[1,16,4,1024]{3,2,0,1:T(4,128)(2,1)}), bf16[1,16,4,1024]{3,2,0,1:T(4,128)(2,1)S(1)}, u32[]{:S(2)}, u32[]{:S(2)}) %all-to-all-start.1) | async-done | bytes 131104 | tf_op jit(solution)/shard_map/all_to_all | solution.py:65
  353.3 0.7 gather_fusion.1
  354.0 0.8 broadcast_select_fusion
  (15 shorter events, 0.0 us)
Async XLA Ops:
  7.2 2.1 copy-start
  7.2 69.3 %all-gather.2.cloned.1.call-start = ((), (), s32[]{:S(2)}) async-start(), calls=%async_computation.3 | async-start | bytes 4456448 | tf_op jit(solution)/shard_map/all_gather | solution.py:41
  7.9 147.3 %reduce-scatter.7.cloned.1.call-start = ((), (), s32[]{:S(2)}) async-start(), calls=%async_computation.5 | async-start | bytes 4456448
  76.4 83.8 %copy-start.2 = (f32[1,1024,64]{1,2,0:T(8,128)S(1)}, f32[1,1024,64]{1,2,0:T(8,128)}, u32[]{:S(2)}) copy-start(f32[1,1024,64]{1,2,0:T(8,128)} %param.7) | copy-start | bytes 786436
  76.4 214.5 %all-reduce.5.cloned.1.call-start = ((), (), s32[]{:S(2)}) async-start(), calls=%async_computation.4 | async-start | bytes 8388608
  176.2 0.7 copy-start.5
  176.2 1.9 copy-start.1
  176.3 150.1 %copy-start.3 = (f32[1,64,1024]{2,1,0:T(8,128)S(1)}, f32[1,64,1024]{2,1,0:T(8,128)}, u32[]{:S(2)}) copy-start(f32[1,64,1024]{2,1,0:T(8,128)} %param.9) | copy-start | bytes 786436
  176.3 167.9 %copy-start.4 = (s32[16]{0:T(128)S(1)}, s32[16]{0:T(128)}, u32[]{:S(2)}) copy-start(s32[16]{0:T(128)} %param.6) | copy-start | bytes 196
  329.2 24.1 %all-to-all-start.1 = ((bf16[1,16,4,1024]{3,2,0,1:T(4,128)(2,1)}), bf16[1,16,4,1024]{3,2,0,1:T(4,128)(2,1)S(1)}, u32[]{:S(2)}, u32[]{:S(2)}) async-start(bf16[1,16,4,1024]{3,2,0,1:T(4,128)(2,1)} %bitcast.12), calls=%async_computation.1 | async-start | bytes 262144 | tf_op jit(solution)/shard_map/all_to_all | solution.py:65
Sparse Core Ops, SparseCore 0:
  10.4 60.3 all-gather.1
  76.6 78.6 reduce-scatter.6
  176.4 114.4 all-reduce.4
where the time goes:
time: 362 us; the launch traced here: 361 us
  waiting for transfers between devices  200 us (55%)
  blocking collectives  92.8 us (26%)
  local copies, waits for them, and re-layouts  17 us (5%)
  between operations  15.9 us (4%)
  starting transfers between devices  15.1 us (4%)
  other arithmetic  10.6 us (3%)
  matrix products  10 us (3%)
    unnamed x5, waiting for transfers between devices  192 us
    all_to_all x1, blocking collectives, body(): lax.all_to_all(arranged, 'shard', split_axis=1, concat_axis=1, tiled=True)  60.8 us
    psum x1, blocking collectives, body(): grad_total = lax.psum(grad_sq, 'dp')  32 us
    all_to_all x1, starting transfers between devices, body(): lax.all_to_all(outgoing, 'shard', split_axis=1, concat_axis=0, tiled=True)  14.9 us
    transpose x1, local copies, waits for them, and re-layouts, body(): jnp.einsum('bic,bcj->ibj', left_roots, right_part, precision=lax.Precisio...  11 us
    all_to_all x1, waiting for transfers between devices, body(): lax.all_to_all(outgoing, 'shard', split_axis=1, concat_axis=0, tiled=True)  8.38 us
  transfers between devices with their start and end apart: 4, of which 3 were waited for; matrix products, arithmetic and copies ran while one was open for 3% of the time, Pallas kernels for 0%

commit v1 on v0

v1 whole, which is shorter than its diff:
```python
import jax
import jax.numpy as jnp
from jax import lax
from jax.experimental import pallas as pl
from jax.experimental.pallas import tpu as pltpu
from jax.sharding import PartitionSpec as P

epsilon = 1e-06
decay_rate = 0.9

MESH = pl.DeviceIdType.MESH
BF = jnp.bfloat16
F32 = jnp.float32
CHUNKS = 4
OFFSETS = (4, 3, 5, 2, 6, 1, 7, 0)
NT = (((1,), (1,)), ((), ()))
NN = (((1,), (0,)), ((), ()))


def split(value):
    high = value.astype(BF)
    return high, (value - high.astype(F32)).astype(BF)


def dot(a, b, dims):
    return lax.dot_general(a, b, dims, preferred_element_type=F32)


def fold(value):
    rows = value.reshape(32, 8, 256).sum(axis=0)
    return rows[:, :128] + rows[:, 128:]


def kernel(
    gp, own, lr, rr, mo, dir_o, nm_o,
    gv, lv, rv, mv, stx, sty, r1x, r1y, s1x, s1y, r2x, r2y, zt, buf_y, buf_x, lg, rg,
    pt, pr, scx, scy, h32, hb, fin, ob, nm,
    loc, s1s, s1r, s2s, s2r, zs, zr, ls, lrc, rs, rrc, gys, gyr, gxs, gxr, ts, tr,
    cxs, cxr, cys, cyr, fs, fr,
):
    dp = lax.axis_index("dp")
    shard = lax.axis_index("shard")
    x, y = lax.rem(dp, 4), lax.div(dp, 4)
    z, core = lax.div(shard, 2), lax.rem(shard, 2)

    def xp(k):
        return lax.rem(x + k, 4)

    def yp(k):
        return lax.rem(y + k, 4)

    def to_x(k):
        return {"dp": y * 4 + xp(k)}

    def to_y(k):
        return {"dp": yp(k) * 4 + x}

    def remote(src, dst, ssem, rsem, device):
        return pltpu.make_async_remote_copy(
            src_ref=src, dst_ref=dst, send_sem=ssem, recv_sem=rsem, device_id=device, device_id_type=MESH
        )

    load_g = pltpu.make_async_copy(gp.at[0], gv, loc.at[0])
    load_l = pltpu.make_async_copy(lr.at[0], lv, loc.at[1])
    load_r = pltpu.make_async_copy(rr.at[0], rv, loc.at[2])
    load_m = pltpu.make_async_copy(mo.at[0], mv, loc.at[3])
    load_g.start()
    load_l.start()
    load_r.start()
    load_m.start()

    barrier = pltpu.get_barrier_semaphore()
    for k in range(1, 4):
        pl.semaphore_signal(barrier, inc=1, device_id=to_x(k), device_id_type=MESH)
        pl.semaphore_signal(barrier, inc=1, device_id=to_y(k), device_id_type=MESH)
    for k in range(1, 16):
        pl.semaphore_signal(
            barrier, inc=1, device_id={"shard": lax.rem(shard + k, 16)}, device_id_type=MESH
        )

    def block_of(slot):
        found = jnp.int32(0)
        for b in range(16):
            found = jnp.where(own[b] == slot, b, found)
        return found

    def stage(q):
        zq = lax.rem(z + OFFSETS[q], 8)
        first = gv[block_of(zq * 2)]
        for i in range(4):
            stx[i, q] = first[16 * i : 16 * i + 16]
        second = gv[block_of(zq * 2 + 1)]
        for j in range(4):
            sty[j, q] = second[:, 256 * j : 256 * j + 256]

    def stage1(c):
        part = pl.ds(2 * c, 2)
        out = []
        for k in range(1, 4):
            out.append(remote(stx.at[xp(k), part], r1x.at[k - 1, part], s1s.at[k - 1, c, 0], s1r.at[k - 1, c, 0], to_x(k)))
            out.append(remote(sty.at[yp(k), part], r1y.at[k - 1, part], s1s.at[k - 1, c, 1], s1r.at[k - 1, c, 1], to_y(k)))
        return out

    def stage2(c):
        part = pl.ds(2 * c, 2)
        out = []
        for k in range(1, 4):
            out.append(remote(s1x.at[yp(k), part], r2x.at[k - 1, part], s2s.at[k - 1, c, 0], s2r.at[k - 1, c, 0], to_y(k)))
            out.append(remote(s1y.at[xp(k), part], r2y.at[k - 1, part], s2s.at[k - 1, c, 1], s2r.at[k - 1, c, 1], to_x(k)))
        return out

    def start_all(copies):
        for copy in copies:
            copy.start()

    def recv_all(copies):
        for copy in copies:
            copy.wait_recv()

    def send_all(copies):
        for copy in copies:
            copy.wait_send()

    def sum1(q):
        total = stx[x, q].astype(F32)
        for k in range(3):
            total = total + r1x[k, q].astype(F32)
        for j in range(4):
            s1x[j, q] = total[:, 256 * j : 256 * j + 256]
        total = sty[y, q].astype(F32)
        for k in range(3):
            total = total + r1y[k, q].astype(F32)
        for i in range(4):
            s1y[i, q] = total[16 * i : 16 * i + 16]

    def sum2(q):
        total = s1x[y, q]
        for k in range(3):
            total = total + r2x[k, q]
        zt[0, q, 0], zt[0, q, 1] = split(total)
        total = s1y[x, q]
        for k in range(3):
            total = total + r2y[k, q]
        zt[1, q, 0], zt[1, q, 1] = split(total)

    def exchange(q, target):
        dst = buf_y.at[y, :, shard] if target == 0 else buf_x.at[:, shard, x]
        device = {"shard": lax.rem(z + OFFSETS[q], 8) * 2 + target}
        return remote(zt.at[target, q], dst, zs.at[target, q], zr.at[q, core], device)

    load_g.wait()
    stage(0)
    stage(1)
    pl.semaphore_wait(barrier, 21)
    start_all(stage1(0))
    for c in range(1, CHUNKS):
        stage(2 * c)
        stage(2 * c + 1)
        start_all(stage1(c))

    def finish2(c):
        recv_all(stage2(c))
        sum2(2 * c)
        sum2(2 * c + 1)
        for q in (2 * c, 2 * c + 1):
            if OFFSETS[q]:
                exchange(q, 0).start()
                exchange(q, 1).start()
            else:
                @pl.when(core == 0)
                def _():
                    exchange(q, 1).start()
                    buf_y[y, :, shard] = zt[0, q]

                @pl.when(core == 1)
                def _():
                    exchange(q, 0).start()
                    buf_x[:, shard, x] = zt[1, q]

    load_l.wait()
    load_r.wait()
    left = split(lv[...])
    right = split(rv[...])
    for h in range(2):
        lg[y, h] = left[h]
        rg[x, h] = right[h]
    roots = []
    for k in range(1, 4):
        roots.append(remote(lg.at[y], lg.at[y], ls.at[k - 1], lrc.at[k - 1], to_y(k)))
        roots.append(remote(rg.at[x], rg.at[x], rs.at[k - 1], rrc.at[k - 1], to_x(k)))

    for c in range(CHUNKS):
        recv_all(stage1(c))
        sum1(2 * c)
        sum1(2 * c + 1)
        start_all(stage2(c))
        if c:
            finish2(c - 1)
    start_all(roots)
    finish2(CHUNKS - 1)

    for c in range(CHUNKS):
        send_all(stage1(c))
        send_all(stage2(c))

    def received(q, source):
        @pl.when(core == 0)
        def _():
            remote(zt.at[0, q], buf_y.at[y, :, shard], zs.at[0, q], zr.at[q, source], {"shard": shard}).wait_recv()

        @pl.when(core == 1)
        def _():
            remote(zt.at[1, q], buf_x.at[:, shard, x], zs.at[1, q], zr.at[q, source], {"shard": shard}).wait_recv()

    for q in range(8):
        if OFFSETS[q]:
            received(q, 0)
            received(q, 1)
        else:
            received(q, 1 - core)

    def gather_y():
        return [remote(buf_y.at[y], buf_y.at[y], gys.at[k - 1], gyr.at[k - 1], to_y(k)) for k in range(1, 4)]

    def gather_x():
        return [
            remote(buf_x.at[:, :, x], buf_x.at[:, :, x], gxs.at[k - 1], gxr.at[k - 1], to_x(k)) for k in range(1, 4)
        ]

    def times_right():
        total = None
        for j in range(4):
            cols = slice(256 * j, 256 * j + 256)
            a_high = buf_y[j, 0].reshape(256, 256)
            a_low = buf_y[j, 1].reshape(256, 256)
            b_high = rg[:, 0, :, cols].reshape(256, 256)
            b_low = rg[:, 1, :, cols].reshape(256, 256)
            part = dot(a_high, b_high, NT) + dot(a_high, b_low, NT) + dot(a_low, b_high, NT)
            total = part if total is None else total + part
        return total

    def left_times():
        a_high = lg[:, 0].reshape(256, 1024)
        a_low = lg[:, 1].reshape(256, 1024)
        b_high = buf_x[0].reshape(1024, 256)
        b_low = buf_x[1].reshape(1024, 256)
        return dot(a_high, b_high, NN) + dot(a_high, b_low, NN) + dot(a_low, b_high, NN)

    lefts, rights = roots[0::2], roots[1::2]

    def finish(tile):
        scx[x, 1] = fold(tile * tile)
        for j in range(4):
            pt[j] = tile[64 * j : 64 * j + 64]

    @pl.when(core == 0)
    def _():
        start_all(gather_y())
        own_tile = (buf_y[y, 0].astype(F32) + buf_y[y, 1].astype(F32)).reshape(256, 256)
        scx[x, 0] = fold(own_tile * own_tile)
        recv_all(rights)
        recv_all(gather_y())
        high, low = split(times_right())
        buf_x[0, :, x] = high.reshape(16, 16, 256)
        buf_x[1, :, x] = low.reshape(16, 16, 256)
        start_all(gather_x())
        recv_all(lefts)
        recv_all(gather_x())
        finish(left_times())

    @pl.when(core == 1)
    def _():
        start_all(gather_x())
        own_tile = (buf_x[0, :, x].astype(F32) + buf_x[1, :, x].astype(F32)).reshape(256, 256)
        scx[x, 0] = fold(own_tile * own_tile)
        recv_all(lefts)
        recv_all(gather_x())
        high, low = split(left_times())
        buf_y[y, 0] = high.reshape(16, 16, 256)
        buf_y[y, 1] = low.reshape(16, 16, 256)
        start_all(gather_y())
        recv_all(rights)
        recv_all(gather_y())
        finish(times_right())

    norms_x = [remote(scx.at[x], scx.at[x], cxs.at[k - 1], cxr.at[k - 1], to_x(k)) for k in range(1, 4)]
    norms_y = [remote(scy.at[y], scy.at[y], cys.at[k - 1], cyr.at[k - 1], to_y(k)) for k in range(1, 4)]
    turn = [remote(pt.at[yp(k)], pr.at[y], ts.at[k - 1], tr.at[k - 1], to_y(k)) for k in range(1, 4)]
    start_all(norms_x)
    start_all(turn)
    pr[y] = pt[y]
    load_m.wait()
    send_all(gather_x())
    send_all(gather_y())
    send_all(roots)
    recv_all(norms_x)
    scy[y] = scx[0] + scx[1] + scx[2] + scx[3]
    start_all(norms_y)
    recv_all(turn)
    recv_all(norms_y)
    sums = scy[0] + scy[1] + scy[2] + scy[3]
    entries = 1024 * 1024
    grad_total = jnp.sum(sums[0], keepdims=True)
    prec_total = jnp.sum(sums[1], keepdims=True)
    scale = jnp.sqrt(grad_total / entries + epsilon) / jnp.sqrt(prec_total / entries + epsilon)
    for j in range(4):
        cols = slice(256 * j, 256 * j + 256)
        graft = pr[j] * scale
        moved = decay_rate * mv[:, cols] + graft
        nm[:, cols] = moved
        heading = decay_rate * moved + graft
        h32[pl.ds(2 * j, 64, stride=8), :] = heading[:, :128]
        h32[pl.ds(2 * j + 1, 64, stride=8), :] = heading[:, 128:]
    hb[...] = h32[...].reshape(16, 32, 128).astype(BF)

    def back(k):
        to = lax.rem(shard + k, 16)
        return remote(hb.at[to], fin.at[shard], fs.at[k], fr.at[k], {"shard": to})

    order = (8, 9, 7, 10, 6, 11, 5, 12, 4, 13, 3, 14, 2, 15, 1)
    for k in order:
        back(k).start()
    store_m = pltpu.make_async_copy(nm, nm_o.at[0], loc.at[4])
    store_m.start()
    fin[shard] = hb[shard]
    send_all(norms_x)
    send_all(norms_y)
    send_all(turn)
    for q in range(8):
        if OFFSETS[q]:
            exchange(q, 0).wait_send()
            exchange(q, 1).wait_send()
        else:
            @pl.when(core == 0)
            def _():
                exchange(q, 1).wait_send()

            @pl.when(core == 1)
            def _():
                exchange(q, 0).wait_send()

    for k in order:
        back(k).wait_recv()
    for b in range(16):
        ob[b] = fin[own[b]]
    store_d = pltpu.make_async_copy(ob, dir_o, loc.at[5])
    store_d.start()
    for k in order:
        back(k).wait_send()
    store_m.wait()
    store_d.wait()


def body(grad_partial, owner_slots, left_roots, right_roots, momentum):
    dma = pltpu.SemaphoreType.DMA
    any_space = pl.BlockSpec(memory_space=pl.ANY)
    direction, new_momentum = pl.pallas_call(
        kernel,
        out_shape=(
            jax.ShapeDtypeStruct((16, 32, 128), BF),
            jax.ShapeDtypeStruct((1, 64, 1024), F32),
        ),
        in_specs=[any_space, pl.BlockSpec(memory_space=pltpu.SMEM), any_space, any_space, any_space],
        out_specs=(any_space, any_space),
        scratch_shapes=[
            pltpu.VMEM((16, 64, 1024), BF),
            pltpu.VMEM((64, 1024), F32),
            pltpu.VMEM((64, 1024), F32),
            pltpu.VMEM((64, 1024), F32),
            pltpu.VMEM((4, 8, 16, 1024), BF),
            pltpu.VMEM((4, 8, 64, 256), BF),
            pltpu.VMEM((3, 8, 16, 1024), BF),
            pltpu.VMEM((3, 8, 64, 256), BF),
            pltpu.VMEM((4, 8, 16, 256), F32),
            pltpu.VMEM((4, 8, 16, 256), F32),
            pltpu.VMEM((3, 8, 16, 256), F32),
            pltpu.VMEM((3, 8, 16, 256), F32),
            pltpu.VMEM((2, 8, 2, 16, 256), BF),
            pltpu.VMEM((4, 2, 16, 16, 256), BF),
            pltpu.VMEM((2, 16, 4, 16, 256), BF),
            pltpu.VMEM((4, 2, 64, 1024), BF),
            pltpu.VMEM((4, 2, 64, 1024), BF),
            pltpu.VMEM((4, 64, 256), F32),
            pltpu.VMEM((4, 64, 256), F32),
            pltpu.VMEM((4, 2, 8, 128), F32),
            pltpu.VMEM((4, 2, 8, 128), F32),
            pltpu.VMEM((512, 128), F32),
            pltpu.VMEM((16, 32, 128), BF),
            pltpu.VMEM((16, 32, 128), BF),
            pltpu.VMEM((16, 32, 128), BF),
            pltpu.VMEM((64, 1024), F32),
            dma((6,)),
            dma((3, 4, 2)), dma((3, 4, 2)),
            dma((3, 4, 2)), dma((3, 4, 2)),
            dma((2, 8)), dma((8, 2)),
            dma((3,)), dma((3,)), dma((3,)), dma((3,)),
            dma((3,)), dma((3,)), dma((3,)), dma((3,)),
            dma((3,)), dma((3,)),
            dma((3,)), dma((3,)), dma((3,)), dma((3,)),
            dma((16,)), dma((16,)),
        ],
        compiler_params=pltpu.CompilerParams(
            collective_id=0, has_side_effects=True, vmem_limit_bytes=60 * 2**20
        ),
    )(grad_partial, owner_slots, jnp.swapaxes(left_roots, 1, 2), right_roots, momentum)
    return direction.reshape(16, 4, 1024), new_momentum


def solution(mesh):
    return jax.shard_map(
        body,
        mesh=mesh,
        in_specs=(
            P("dp", None, "shard", None),
            P(),
            P("shard", None, "dp"),
            P("shard", "dp", None),
            P("shard", "dp", None),
        ),
        out_specs=(P(None, ("dp", "shard"), None), P("shard", "dp", None)),
        check_vma=False,
    )
```

time: 362 us -> 78.5 us (0.22)
  waiting for transfers between devices: 200 us -> 0 us
  blocking collectives: 92.8 us -> 0 us
  Pallas kernels: 0 us -> 74.4 us
  between operations: 15.9 us -> 0.64 us
  starting transfers between devices: 15.1 us -> 0 us
  local copies, waits for them, and re-layouts: 17 us -> 3.26 us
  other arithmetic: 10.6 us -> 0 us
  matrix products: 10 us -> 0 us
    unnamed x5 -> x0, waiting for transfers between devices: 192 us -> none
    pallas_call x0 -> x1, Pallas kernels: none -> 74.4 us  [body(): pl.pallas_call(kernel, out_shape=(jax.ShapeDtypeStruct((16, 32, 128), BF)...]
    all_to_all x1 -> x0, blocking collectives: 60.8 us -> none  [body(): lax.all_to_all(arranged, 'shard', split_axis=1, concat_axis=1, tiled=True)]
    psum x1 -> x0, blocking collectives: 32 us -> none  [body(): grad_total = lax.psum(grad_sq, 'dp')]
    all_to_all x1 -> x0, starting transfers between devices: 14.9 us -> none  [body(): lax.all_to_all(outgoing, 'shard', split_axis=1, concat_axis=0, tiled=True)]
    transpose x1 -> x0, local copies, waits for them, and re-layouts: 11 us -> none  [body(): jnp.einsum('bic,bcj->ibj', left_roots, right_part, precision=lax.Precisio...]
    dot_general x2 -> x0, matrix products: 10 us -> none  [the longest x1 5.09 us: body(): jnp.einsum('bic,bcj->ibj', left_roots, right_part, precision=lax.Precisio...]
    all_to_all x1 -> x0, waiting for transfers between devices: 8.38 us -> none  [body(): lax.all_to_all(outgoing, 'shard', split_axis=1, concat_axis=0, tiled=True)]
  transfers between devices with their start and end apart: 4 -> 0, of which waited for: 3 -> 0; matrix products, arithmetic and copies ran while one was open for 3% -> 0% of each run, Pallas kernels for 0% -> 0%
where the time goes in v1:
time: 78.5 us; the launch traced here: 78.3 us
  Pallas kernels  74.4 us (95%)
  local copies, waits for them, and re-layouts  3.26 us (4%)
    pallas_call x1, Pallas kernels, body(): pl.pallas_call(kernel, out_shape=(jax.ShapeDtypeStruct((16, 32, 128), BF)...  74.4 us
    unnamed x1, local copies, waits for them, and re-layouts  1.67 us
    reshape x1, local copies, waits for them, and re-layouts, body(): return (direction.reshape(16, 4, 1024), new_momentum)  1.59 us

profile of v1, /device:TPU:1, one launch (start us, length us, event | category | flops | bytes accessed | tf_op | source)
XLA Modules:
  0.0 78.3 jit_solution(13571011760039114687)
XLA Ops:
  0.6 74.4 %shard_map.68 = (bf16[16,32,128]{2,1,0:T(8,128)(2,1)}, f32[1,64,1024]{2,1,0:T(8,128)}) custom-call(bf16[1,16,64,1024]{3,2,1,0:T(8,128)(2,1)} %gp.1, s32[16]{0:T(128)} %own.1, f32[1,64,1024]{2,1,0:T(8,128)} %bitcast.1, f32[1,64,1024]{2,1,0:T(8,128)} %rr.1, f32[1,64,1024]{2,1,0:T(8,128)} %mo.1), custom_call_target="tpu_custom_call" | custom-call | tf_op jit(solution)/shard_map/pallas_call | solution.py:357
  75.0 1.6 %reshape.7 = bf16[16,4,1024]{2,1,0:T(4,128)(2,1)} reshape(bf16[16,32,128]{2,1,0:T(8,128)(2,1)} %get-tuple-element.4) | data formatting | bytes 262144 | tf_op jit(solution)/shard_map/reshape | solution.py:406
  76.6 1.7 %copy.8 = f32[1,64,1024]{2,1,0:T(8,128)} copy(f32[1,64,1024]{2,1,0:T(8,128)} %get-tuple-element.9) | data formatting | bytes 524288

commit v2 on v1

v2 whole, which is shorter than its diff:
```python
import jax
import jax.numpy as jnp
from jax import lax
from jax.experimental import pallas as pl
from jax.experimental.pallas import tpu as pltpu
from jax.sharding import PartitionSpec as P

epsilon = 1e-06
decay_rate = 0.9

MESH = pl.DeviceIdType.MESH
BF = jnp.bfloat16
F32 = jnp.float32
CHUNKS = 4
OFFSETS = (4, 3, 5, 2, 6, 1, 7, 0)
PASS1 = (True, True, True, True, True, True, False, False)
PASS2 = (True, True, True, True, True, True, False, False)
PASSR = True
PASSL = True
NT = (((1,), (1,)), ((), ()))
NN = (((1,), (0,)), ((), ()))


def split(value):
    high = value.astype(BF)
    return high, (value - high.astype(F32)).astype(BF)


def dot(a, b, dims):
    return lax.dot_general(a, b, dims, preferred_element_type=F32)


def fold(value):
    rows = value.reshape(32, 8, 256).sum(axis=0)
    return rows[:, :128] + rows[:, 128:]


def kernel(
    gp, own, lr, rr, mo, dir_o, nm_o,
    gv, lv, rv, mv, stx, sty, r1x, r1y, s1x, s1y, r2x, r2y, zt, gbuf, hbuf, lg, rg,
    pt, pr, scx, scy, h32, hb, fin, ob, nm,
    loc, s1s, s1r, s2s, s2r, zs, zr, ls, lrc, rs, rrc, g1s, g1r, g2s, g2r, ts, tr,
    cxs, cxr, cys, cyr, fs, fr,
):
    dp = lax.axis_index("dp")
    shard = lax.axis_index("shard")
    x, y = lax.rem(dp, 4), lax.div(dp, 4)
    z, core = lax.div(shard, 2), lax.rem(shard, 2)
    u = (1 - core) * x + core * y
    v = (1 - core) * y + core * x

    def step(i, k):
        return lax.rem(i + k, 4)

    def to_x(k):
        return {"dp": y * 4 + step(x, k)}

    def to_y(k):
        return {"dp": step(y, k) * 4 + x}

    def to_u(k):
        return {"dp": (1 - core) * (y * 4 + step(x, k)) + core * (step(y, k) * 4 + x)}

    def to_v(k):
        return {"dp": core * (y * 4 + step(x, k)) + (1 - core) * (step(y, k) * 4 + x)}

    def remote(src, dst, ssem, rsem, device):
        return pltpu.make_async_remote_copy(
            src_ref=src, dst_ref=dst, send_sem=ssem, recv_sem=rsem, device_id=device, device_id_type=MESH
        )

    def start_all(copies):
        for copy in copies:
            copy.start()

    def recv_all(copies):
        for copy in copies:
            copy.wait_recv()

    def send_all(copies):
        for copy in copies:
            copy.wait_send()

    load_g = pltpu.make_async_copy(gp.at[0], gv, loc.at[0])
    load_l = pltpu.make_async_copy(lr.at[0], lv, loc.at[1])
    load_r = pltpu.make_async_copy(rr.at[0], rv, loc.at[2])
    load_m = pltpu.make_async_copy(mo.at[0], mv, loc.at[3])
    load_g.start()
    load_r.start()
    load_l.start()
    load_m.start()

    barrier = pltpu.get_barrier_semaphore()
    for k in range(1, 4):
        pl.semaphore_signal(barrier, inc=1, device_id=to_x(k), device_id_type=MESH)
        pl.semaphore_signal(barrier, inc=1, device_id=to_y(k), device_id_type=MESH)
    for k in range(1, 16):
        pl.semaphore_signal(
            barrier, inc=1, device_id={"shard": lax.rem(shard + k, 16)}, device_id_type=MESH
        )

    def block_of(slot):
        found = jnp.int32(0)
        for b in range(16):
            found = jnp.where(own[b] == slot, b, found)
        return found

    def stage(q):
        zq = lax.rem(z + OFFSETS[q], 8)
        for target, staged in enumerate((stx, sty)):
            block = gv[block_of(zq * 2 + target)]
            for i in range(4):
                staged[i, q] = block[16 * i : 16 * i + 16]

    def stage1(c):
        part = pl.ds(2 * c, 2)
        out = []
        for k in range(1, 4):
            out.append(remote(stx.at[step(x, k), part], r1x.at[k - 1, part], s1s.at[k - 1, c, 0], s1r.at[k - 1, c, 0], to_x(k)))
            out.append(remote(sty.at[step(y, k), part], r1y.at[k - 1, part], s1s.at[k - 1, c, 1], s1r.at[k - 1, c, 1], to_y(k)))
        return out

    def sum1(q):
        for staged, got, summed, me in ((stx, r1x, s1x, x), (sty, r1y, s1y, y)):
            total = staged[me, q].astype(F32)
            for k in range(3):
                total = total + got[k, q].astype(F32)
            for j in range(4):
                summed[j, q] = total[:, 256 * j : 256 * j + 256]

    def stage2(c):
        part = pl.ds(2 * c, 2)
        out = []
        for k in range(1, 4):
            out.append(remote(s1x.at[step(y, k), part], r2x.at[k - 1, part], s2s.at[k - 1, c, 0], s2r.at[k - 1, c, 0], to_y(k)))
            out.append(remote(s1y.at[step(x, k), part], r2y.at[k - 1, part], s2s.at[k - 1, c, 1], s2r.at[k - 1, c, 1], to_x(k)))
        return out

    def sum2(q):
        for target, (summed, got, me) in enumerate(((s1x, r2x, y), (s1y, r2y, x))):
            total = summed[me, q]
            for k in range(3):
                total = total + got[k, q]
            zt[target, q, 0], zt[target, q, 1] = split(total)

    def exchange(q, target):
        dst = gbuf.at[shard, y if target == 0 else x]
        device = {"shard": lax.rem(z + OFFSETS[q], 8) * 2 + target}
        return remote(zt.at[target, q], dst, zs.at[target, q], zr.at[q, core], device)

    def send_z(q):
        if OFFSETS[q]:
            exchange(q, 0).start()
            exchange(q, 1).start()
        else:
            @pl.when(core == 0)
            def _():
                exchange(q, 1).start()
                gbuf[shard, y] = zt[0, q]

            @pl.when(core == 1)
            def _():
                exchange(q, 0).start()
                gbuf[shard, x] = zt[1, q]

    def wait_z(q):
        for source in range(2):
            def wait():
                remote(zt.at[0, q], gbuf.at[shard, v], zs.at[0, q], zr.at[q, source], {"shard": shard}).wait_recv()

            if OFFSETS[q]:
                wait()
            else:
                pl.when(core != source)(wait)

    def sent_z(q):
        if OFFSETS[q]:
            exchange(q, 0).wait_send()
            exchange(q, 1).wait_send()
        else:
            pl.when(core == 0)(lambda: exchange(q, 1).wait_send())
            pl.when(core == 1)(lambda: exchange(q, 0).wait_send())

    def pair(q):
        return pl.ds(2 * lax.rem(z + 8 - OFFSETS[q], 8), 2)

    class Gather:
        def __init__(self, piece, half, me, to, ssem, rsem, passing):
            own_piece = piece(me)
            self.direct = [
                remote(own_piece, own_piece, ssem.at[0], rsem.at[0], to(1)),
                remote(own_piece, own_piece, ssem.at[1], rsem.at[1], to(3)),
            ]
            if passing:
                after, before = half(step(me, 3), 0), half(step(me, 1), 1)
                self.passed = [
                    remote(after, after, ssem.at[2], rsem.at[2], to(1)),
                    remote(before, before, ssem.at[3], rsem.at[3], to(3)),
                ]
            else:
                self.passed = [remote(own_piece, own_piece, ssem.at[2], rsem.at[2], to(2))]
            self.passing = passing

        def start(self):
            start_all(self.direct)
            if not self.passing:
                start_all(self.passed)

        def go_on(self):
            if self.passing:
                for received, onward in zip(self.direct, self.passed):
                    received.wait_recv()
                    onward.start()

        def wait(self):
            if not self.passing:
                recv_all(self.direct)
            recv_all(self.passed)

        def sent(self):
            send_all(self.direct)
            send_all(self.passed)

    def gather1(q):
        return Gather(
            lambda i: gbuf.at[pair(q), i], lambda i, h: gbuf.at[pair(q), i, h], v, to_v, g1s.at[q], g1r.at[q], PASS1[q]
        )

    def gather2(q):
        return Gather(
            lambda i: hbuf.at[:, pair(q), i], lambda i, h: hbuf.at[h, pair(q), i], u, to_u, g2s.at[q], g2r.at[q], PASS2[q]
        )

    def times_right(q):
        total = None
        for j in range(4):
            cols = slice(256 * j, 256 * j + 256)
            high, low = (
                jnp.concatenate([gbuf[pair(i), j, h].reshape(32, 256) for i in (q, q + 1)], axis=0) for h in range(2)
            )
            b_high = rg[:, 0, :, cols].reshape(256, 256)
            b_low = rg[:, 1, :, cols].reshape(256, 256)
            both = dot(jnp.concatenate([high, low], axis=0), b_high, NT)
            part = both[:64] + both[64:] + dot(high, b_low, NT)
            total = part if total is None else total + part
        high, low = split(total)
        for i in range(2):
            hbuf[0, pair(q + i), u] = high[32 * i : 32 * i + 32].reshape(2, 16, 256)
            hbuf[1, pair(q + i), u] = low[32 * i : 32 * i + 32].reshape(2, 16, 256)

    def left_times():
        a_high = lg[:, 0].reshape(256, 1024)
        a_low = lg[:, 1].reshape(256, 1024)
        b_high = hbuf[0].reshape(1024, 256)
        b_low = hbuf[1].reshape(1024, 256)
        return dot(a_high, b_high, NN) + dot(a_high, b_low, NN) + dot(a_low, b_high, NN)

    rights = Gather(lambda i: rg.at[i], lambda i, h: rg.at[i, h], u, to_u, rs, rrc, PASSR)
    lefts = Gather(lambda i: lg.at[i], lambda i, h: lg.at[i, h], v, to_v, ls, lrc, PASSL)

    load_g.wait()
    stage(0)
    stage(1)
    pl.semaphore_wait(barrier, 21)
    start_all(stage1(0))
    for c in range(1, CHUNKS):
        stage(2 * c)
        stage(2 * c + 1)
        start_all(stage1(c))

    load_r.wait()
    rg[u, 0], rg[u, 1] = split(rv[...])
    load_l.wait()
    lg[v, 0], lg[v, 1] = split(lv[...])

    def sum_first(c):
        recv_all(stage1(c))
        sum1(2 * c)
        sum1(2 * c + 1)
        start_all(stage2(c))

    def sum_second(c):
        recv_all(stage2(c))
        for q in (2 * c, 2 * c + 1):
            sum2(q)
            send_z(q)

    def spread_rows(c):
        for q in (2 * c, 2 * c + 1):
            wait_z(q)
            gather1(q).start()

    def pass_rows(c):
        for q in (2 * c, 2 * c + 1):
            gather1(q).go_on()

    def multiply_right(c):
        for q in (2 * c, 2 * c + 1):
            gather1(q).wait()
        times_right(2 * c)
        for q in (2 * c, 2 * c + 1):
            gather2(q).start()

    def pass_products(c):
        for q in (2 * c, 2 * c + 1):
            gather2(q).go_on()

    def wait_products(c):
        for q in (2 * c, 2 * c + 1):
            gather2(q).wait()

    def norm_of_gradient():
        tile = gbuf[:, v]
        tile = (tile[:, 0].astype(F32) + tile[:, 1].astype(F32)).reshape(256, 256)
        scx[x, 0] = fold(tile * tile)

    sum_first(0)
    sum_first(1)
    sum_first(2)
    sum_first(3)
    rights.start()
    sum_second(0)
    sum_second(1)
    sum_second(2)
    rights.go_on()
    sum_second(3)
    lefts.start()
    spread_rows(0)
    spread_rows(1)
    spread_rows(2)
    spread_rows(3)
    pass_rows(0)
    pass_rows(1)
    pass_rows(2)
    pass_rows(3)
    norm_of_gradient()
    lefts.go_on()
    rights.wait()
    multiply_right(0)
    multiply_right(1)
    multiply_right(2)
    multiply_right(3)
    pass_products(0)
    pass_products(1)
    pass_products(2)
    pass_products(3)
    lefts.wait()
    wait_products(0)
    wait_products(1)
    wait_products(2)
    wait_products(3)

    tile = left_times()
    scx[x, 1] = fold(tile * tile)
    for j in range(4):
        pt[j] = tile[64 * j : 64 * j + 64]

    norms_x = [remote(scx.at[x], scx.at[x], cxs.at[k - 1], cxr.at[k - 1], to_x(k)) for k in range(1, 4)]
    norms_y = [remote(scy.at[y], scy.at[y], cys.at[k - 1], cyr.at[k - 1], to_y(k)) for k in range(1, 4)]
    turn = [remote(pt.at[step(v, k)], pr.at[v], ts.at[k - 1], tr.at[k - 1], to_v(k)) for k in range(1, 4)]
    start_all(norms_x)
    start_all(turn)
    pr[v] = pt[v]
    load_m.wait()
    for c in range(CHUNKS):
        send_all(stage1(c))
    recv_all(norms_x)
    scy[y] = scx[0] + scx[1] + scx[2] + scx[3]
    start_all(norms_y)
    for c in range(CHUNKS):
        send_all(stage2(c))
    for q in range(8):
        sent_z(q)
    recv_all(turn)
    recv_all(norms_y)
    sums = scy[0] + scy[1] + scy[2] + scy[3]
    entries = 1024 * 1024
    grad_total = jnp.sum(sums[0], keepdims=True)
    prec_total = jnp.sum(sums[1], keepdims=True)
    scale = jnp.sqrt(grad_total / entries + epsilon) / jnp.sqrt(prec_total / entries + epsilon)

    def update(columns):
        for j in range(8):
            cols = slice(128 * j, 128 * j + 128)
            graft = columns(j) * scale
            moved = decay_rate * mv[:, cols] + graft
            nm[:, cols] = moved
            h32[:, cols] = decay_rate * moved + graft

    @pl.when(core == 0)
    def _():
        update(lambda j: pr[j // 2, :, 128 * (j % 2) : 128 * (j % 2) + 128])

    @pl.when(core == 1)
    def _():
        def columns(j):
            strip = slice(64 * (j // 2), 64 * (j // 2) + 64)
            first = 2 * (j % 2)
            return jnp.concatenate([pr[first, :, strip], pr[first + 1, :, strip]], axis=1)

        update(columns)

    hb[...] = h32[...].reshape(16, 4, 1024).astype(BF)

    def back(k):
        to = lax.rem(shard + k, 16)
        return remote(hb.at[to], fin.at[shard], fs.at[k], fr.at[k], {"shard": to})

    order = (8, 9, 7, 10, 6, 11, 5, 12, 4, 13, 3, 14, 2, 15, 1)
    for k in order:
        back(k).start()
    store_m = pltpu.make_async_copy(nm, nm_o.at[0], loc.at[4])
    store_m.start()
    fin[shard] = hb[shard]
    send_all(norms_x)
    send_all(norms_y)
    send_all(turn)
    rights.sent()
    lefts.sent()
    for q in range(8):
        gather1(q).sent()
        gather2(q).sent()
    for k in order:
        back(k).wait_recv()
    for b in range(16):
        ob[b] = fin[own[b]]
    store_d = pltpu.make_async_copy(ob, dir_o, loc.at[5])
    store_d.start()
    for k in order:
        back(k).wait_send()
    store_m.wait()
    store_d.wait()


def last(d_in, m_in, d_out, m_out, sem, d, m):
    loads = [pltpu.make_async_copy(m_in, m, sem.at[0]), pltpu.make_async_copy(d_in, d, sem.at[1])]
    stores = [pltpu.make_async_copy(m, m_out, sem.at[2]), pltpu.make_async_copy(d, d_out, sem.at[3])]
    for copy in loads:
        copy.start()
    for load, store in zip(loads, stores):
        load.wait()
        store.start()
    for copy in stores:
        copy.wait()


def body(grad_partial, owner_slots, left_roots, right_roots, momentum):
    dma = pltpu.SemaphoreType.DMA
    any_space = pl.BlockSpec(memory_space=pl.ANY)
    direction, new_momentum = pl.pallas_call(
        kernel,
        out_shape=(
            jax.ShapeDtypeStruct((16, 4, 1024), BF),
            jax.ShapeDtypeStruct((1, 64, 1024), F32),
        ),
        in_specs=[any_space, pl.BlockSpec(memory_space=pltpu.SMEM), any_space, any_space, any_space],
        out_specs=(any_space, any_space),
        scratch_shapes=[
            pltpu.VMEM((16, 64, 1024), BF),
            pltpu.VMEM((64, 1024), F32),
            pltpu.VMEM((64, 1024), F32),
            pltpu.VMEM((64, 1024), F32),
            pltpu.VMEM((4, 8, 16, 1024), BF),
            pltpu.VMEM((4, 8, 16, 1024), BF),
            pltpu.VMEM((3, 8, 16, 1024), BF),
            pltpu.VMEM((3, 8, 16, 1024), BF),
            pltpu.VMEM((4, 8, 16, 256), F32),
            pltpu.VMEM((4, 8, 16, 256), F32),
            pltpu.VMEM((3, 8, 16, 256), F32),
            pltpu.VMEM((3, 8, 16, 256), F32),
            pltpu.VMEM((2, 8, 2, 16, 256), BF),
            pltpu.VMEM((16, 4, 2, 16, 256), BF),
            pltpu.VMEM((2, 16, 4, 16, 256), BF),
            pltpu.VMEM((4, 2, 64, 1024), BF),
            pltpu.VMEM((4, 2, 64, 1024), BF),
            pltpu.VMEM((4, 64, 256), F32),
            pltpu.VMEM((4, 64, 256), F32),
            pltpu.VMEM((4, 2, 8, 128), F32),
            pltpu.VMEM((4, 2, 8, 128), F32),
            pltpu.VMEM((64, 1024), F32),
            pltpu.VMEM((16, 4, 1024), BF),
            pltpu.VMEM((16, 4, 1024), BF),
            pltpu.VMEM((16, 4, 1024), BF),
            pltpu.VMEM((64, 1024), F32),
            dma((6,)),
            dma((3, 4, 2)), dma((3, 4, 2)),
            dma((3, 4, 2)), dma((3, 4, 2)),
            dma((2, 8)), dma((8, 2)),
            dma((4,)), dma((4,)), dma((4,)), dma((4,)),
            dma((8, 4)), dma((8, 4)), dma((8, 4)), dma((8, 4)),
            dma((3,)), dma((3,)),
            dma((3,)), dma((3,)), dma((3,)), dma((3,)),
            dma((16,)), dma((16,)),
        ],
        compiler_params=pltpu.CompilerParams(
            collective_id=0, has_side_effects=True, vmem_limit_bytes=60 * 2**20
        ),
    )(grad_partial, owner_slots, jnp.swapaxes(left_roots, 1, 2), right_roots, momentum)
    vmem = pl.BlockSpec(memory_space=pltpu.VMEM)
    return pl.pallas_call(
        last,
        out_shape=(
            jax.ShapeDtypeStruct((16, 4, 1024), BF),
            jax.ShapeDtypeStruct((1, 64, 1024), F32),
        ),
        in_specs=[any_space, any_space],
        out_specs=(any_space, any_space),
        scratch_shapes=[dma((4,)), pltpu.VMEM((16, 4, 1024), BF), pltpu.VMEM((1, 64, 1024), F32)],
        compiler_params=pltpu.CompilerParams(vmem_limit_bytes=60 * 2**20),
    )(direction, new_momentum)


def solution(mesh):
    return jax.shard_map(
        body,
        mesh=mesh,
        in_specs=(
            P("dp", None, "shard", None),
            P(),
            P("shard", None, "dp"),
            P("shard", "dp", None),
            P("shard", "dp", None),
        ),
        out_specs=(P(None, ("dp", "shard"), None), P("shard", "dp", None)),
        check_vma=False,
    )
```

time: 78.5 us -> 71.1 us (0.906)
  Pallas kernels: 74.4 us -> 70.3 us
  local copies, waits for them, and re-layouts: 3.26 us -> 0 us
    pallas_call x1 -> x2, Pallas kernels: 74.4 us -> 70.3 us  [the longest x1 68.6 us: body(): pl.pallas_call(kernel, out_shape=(jax.ShapeDtypeStruct((16, 4, 1024), BF)...]
    unnamed x1 -> x0, local copies, waits for them, and re-layouts: 1.67 us -> none
    reshape x1 -> x0, local copies, waits for them, and re-layouts: 1.59 us -> none  [body(): return (direction.reshape(16, 4, 1024), new_momentum)]
where the time goes in v2:
time: 71.1 us; the launch traced here: 71 us
  Pallas kernels  70.3 us (99%)
    pallas_call x1, Pallas kernels, body(): pl.pallas_call(kernel, out_shape=(jax.ShapeDtypeStruct((16, 4, 1024), BF)...  68.6 us
    pallas_call x1, Pallas kernels, body(): pl.pallas_call(last, out_shape=(jax.ShapeDtypeStruct((16, 4, 1024), BF),...  1.73 us

profile of v2, /device:TPU:1, one launch (start us, length us, event | category | flops | bytes accessed | tf_op | source)
XLA Modules:
  0.0 71.0 jit_solution(12662341582029236455)
XLA Ops:
  0.6 68.6 %shard_map.68 = (bf16[16,4,1024]{2,1,0:T(4,128)(2,1)}, f32[1,64,1024]{2,1,0:T(8,128)}) custom-call(bf16[1,16,64,1024]{3,2,1,0:T(8,128)(2,1)} %gp.1, s32[16]{0:T(128)} %own.1, f32[1,64,1024]{2,1,0:T(8,128)} %bitcast.1, f32[1,64,1024]{2,1,0:T(8,128)} %rr.1, f32[1,64,1024]{2,1,0:T(8,128)} %mo.1), custom_call_target="tpu_custom_call" | custom-call | tf_op jit(solution)/shard_map/pallas_call | solution.py:450
  69.2 1.7 %shard_map.69 = (bf16[16,4,1024]{2,1,0:T(4,128)(2,1)}, f32[1,64,1024]{2,1,0:T(8,128)}) custom-call(bf16[16,4,1024]{2,1,0:T(4,128)(2,1)} %get-tuple-element.4.d_in, f32[1,64,1024]{2,1,0:T(8,128)} %get-tuple-element.5.m_in), custom_call_target="tpu_custom_call" | custom-call | tf_op jit(solution)/shard_map/pallas_call | solution.py:500

commit v3 on v2

--- a/solution.py
+++ b/solution.py
@@ -11,7 +11,8 @@
 MESH = pl.DeviceIdType.MESH
 BF = jnp.bfloat16
 F32 = jnp.float32
-CHUNKS = 4
+PARTS = ((0, 2), (2, 2), (4, 2), (6, 2))
+CHUNKS = len(PARTS)
 OFFSETS = (4, 3, 5, 2, 6, 1, 7, 0)
 PASS1 = (True, True, True, True, True, True, False, False)
 PASS2 = (True, True, True, True, True, True, False, False)
@@ -113,7 +114,7 @@
                 staged[i, q] = block[16 * i : 16 * i + 16]
 
     def stage1(c):
-        part = pl.ds(2 * c, 2)
+        part = pl.ds(*PARTS[c])
         out = []
         for k in range(1, 4):
             out.append(remote(stx.at[step(x, k), part], r1x.at[k - 1, part], s1s.at[k - 1, c, 0], s1r.at[k - 1, c, 0], to_x(k)))
@@ -129,7 +130,7 @@
                 summed[j, q] = total[:, 256 * j : 256 * j + 256]
 
     def stage2(c):
-        part = pl.ds(2 * c, 2)
+        part = pl.ds(*PARTS[c])
         out = []
         for k in range(1, 4):
             out.append(remote(s1x.at[step(y, k), part], r2x.at[k - 1, part], s2s.at[k - 1, c, 0], s2r.at[k - 1, c, 0], to_y(k)))
@@ -210,7 +211,7 @@
             if self.passing:
                 for received, onward in zip(self.direct, self.passed):
                     received.wait_recv()
-                    onward.start()
+                    start_all([onward])
 
         def wait(self):
             if not self.passing:
@@ -231,41 +232,48 @@
             lambda i: hbuf.at[:, pair(q), i], lambda i, h: hbuf.at[h, pair(q), i], u, to_u, g2s.at[q], g2r.at[q], PASS2[q]
         )
 
-    def times_right(q):
+    def times_right(qs):
+        rows = 32 * len(qs)
         total = None
         for j in range(4):
             cols = slice(256 * j, 256 * j + 256)
             high, low = (
-                jnp.concatenate([gbuf[pair(i), j, h].reshape(32, 256) for i in (q, q + 1)], axis=0) for h in range(2)
+                jnp.concatenate([gbuf[pair(i), j, h].reshape(32, 256) for i in qs], axis=0) for h in range(2)
             )
             b_high = rg[:, 0, :, cols].reshape(256, 256)
             b_low = rg[:, 1, :, cols].reshape(256, 256)
             both = dot(jnp.concatenate([high, low], axis=0), b_high, NT)
-            part = both[:64] + both[64:] + dot(high, b_low, NT)
+            part = both[:rows] + both[rows:] + dot(high, b_low, NT)
             total = part if total is None else total + part
         high, low = split(total)
-        for i in range(2):
-            hbuf[0, pair(q + i), u] = high[32 * i : 32 * i + 32].reshape(2, 16, 256)
-            hbuf[1, pair(q + i), u] = low[32 * i : 32 * i + 32].reshape(2, 16, 256)
-
-    def left_times():
-        a_high = lg[:, 0].reshape(256, 1024)
-        a_low = lg[:, 1].reshape(256, 1024)
-        b_high = hbuf[0].reshape(1024, 256)
-        b_low = hbuf[1].reshape(1024, 256)
+        for i, q in enumerate(qs):
+            hbuf[0, pair(q), u] = high[32 * i : 32 * i + 32].reshape(2, 16, 256)
+            hbuf[1, pair(q), u] = low[32 * i : 32 * i + 32].reshape(2, 16, 256)
+
+    def left_times(part):
+        high, low = [], []
+        for q in part:
+            cols = pl.ds(pl.multiple_of(128 * lax.rem(z + 8 - OFFSETS[q], 8), 128), 128)
+            high.append(lg[:, 0, :, cols].reshape(256, 128))
+            low.append(lg[:, 1, :, cols].reshape(256, 128))
+        a_high, a_low = (jnp.concatenate(cols, axis=1) for cols in (high, low))
+        b_high, b_low = (
+            jnp.concatenate([hbuf[h, pair(q)].reshape(128, 256) for q in part], axis=0) for h in range(2)
+        )
         return dot(a_high, b_high, NN) + dot(a_high, b_low, NN) + dot(a_low, b_high, NN)
 
     rights = Gather(lambda i: rg.at[i], lambda i, h: rg.at[i, h], u, to_u, rs, rrc, PASSR)
     lefts = Gather(lambda i: lg.at[i], lambda i, h: lg.at[i, h], v, to_v, ls, lrc, PASSL)
 
+    def slots(c):
+        return range(PARTS[c][0], PARTS[c][0] + PARTS[c][1])
+
     load_g.wait()
-    stage(0)
-    stage(1)
-    pl.semaphore_wait(barrier, 21)
-    start_all(stage1(0))
-    for c in range(1, CHUNKS):
-        stage(2 * c)
-        stage(2 * c + 1)
+    for c in range(CHUNKS):
+        for q in slots(c):
+            stage(q)
+        if c == 0:
+            pl.semaphore_wait(barrier, 21)
         start_all(stage1(c))
 
     load_r.wait()
@@ -275,39 +283,41 @@
 
     def sum_first(c):
         recv_all(stage1(c))
-        sum1(2 * c)
-        sum1(2 * c + 1)
+        for q in slots(c):
+            sum1(q)
         start_all(stage2(c))
 
     def sum_second(c):
         recv_all(stage2(c))
-        for q in (2 * c, 2 * c + 1):
+        for q in slots(c):
             sum2(q)
             send_z(q)
 
     def spread_rows(c):
-        for q in (2 * c, 2 * c + 1):
+        for q in slots(c):
             wait_z(q)
             gather1(q).start()
 
     def pass_rows(c):
-        for q in (2 * c, 2 * c + 1):
+        for q in slots(c):
             gather1(q).go_on()
 
     def multiply_right(c):
-        for q in (2 * c, 2 * c + 1):
+        for q in slots(c):
             gather1(q).wait()
-        times_right(2 * c)
-        for q in (2 * c, 2 * c + 1):
+        times_right(slots(c))
+        for q in slots(c):
             gather2(q).start()
 
     def pass_products(c):
-        for q in (2 * c, 2 * c + 1):
+        for q in slots(c):
             gather2(q).go_on()
 
-    def wait_products(c):
-        for q in (2 * c, 2 * c + 1):
+    def multiply_left(c):
+        for q in slots(c):
             gather2(q).wait()
+        product = left_times(slots(c)).reshape(4, 64, 256)
+        pt[...] = product if c == 0 else pt[...] + product
 
     def norm_of_gradient():
         tile = gbuf[:, v]
@@ -345,15 +355,13 @@
     pass_products(2)
     pass_products(3)
     lefts.wait()
-    wait_products(0)
-    wait_products(1)
-    wait_products(2)
-    wait_products(3)
-
-    tile = left_times()
+    multiply_left(0)
+    multiply_left(1)
+    multiply_left(2)
+    multiply_left(3)
+
+    tile = pt[...].reshape(256, 256)
     scx[x, 1] = fold(tile * tile)
-    for j in range(4):
-        pt[j] = tile[64 * j : 64 * j + 64]
 
     norms_x = [remote(scx.at[x], scx.at[x], cxs.at[k - 1], cxr.at[k - 1], to_x(k)) for k in range(1, 4)]
     norms_y = [remote(scy.at[y], scy.at[y], cys.at[k - 1], cyr.at[k - 1], to_y(k)) for k in range(1, 4)]
@@ -384,7 +392,7 @@
             cols = slice(128 * j, 128 * j + 128)
             graft = columns(j) * scale
             moved = decay_rate * mv[:, cols] + graft
-            nm[:, cols] = moved
+            nm_o[0, :, cols] = moved
             h32[:, cols] = decay_rate * moved + graft
 
     @pl.when(core == 0)
@@ -409,8 +417,6 @@
     order = (8, 9, 7, 10, 6, 11, 5, 12, 4, 13, 3, 14, 2, 15, 1)
     for k in order:
         back(k).start()
-    store_m = pltpu.make_async_copy(nm, nm_o.at[0], loc.at[4])
-    store_m.start()
     fin[shard] = hb[shard]
     send_all(norms_x)
     send_all(norms_y)
@@ -423,24 +429,16 @@
     for k in order:
         back(k).wait_recv()
     for b in range(16):
-        ob[b] = fin[own[b]]
-    store_d = pltpu.make_async_copy(ob, dir_o, loc.at[5])
-    store_d.start()
+        dir_o[b] = fin[own[b]]
     for k in order:
         back(k).wait_send()
-    store_m.wait()
-    store_d.wait()
-
-
-def last(d_in, m_in, d_out, m_out, sem, d, m):
-    loads = [pltpu.make_async_copy(m_in, m, sem.at[0]), pltpu.make_async_copy(d_in, d, sem.at[1])]
-    stores = [pltpu.make_async_copy(m, m_out, sem.at[2]), pltpu.make_async_copy(d, d_out, sem.at[3])]
-    for copy in loads:
+
+
+def last(d_in, m_in, d_out, m_out, sem):
+    copies = [pltpu.make_async_copy(m_in, m_out, sem.at[0]), pltpu.make_async_copy(d_in, d_out, sem.at[1])]
+    for copy in copies:
         copy.start()
-    for load, store in zip(loads, stores):
-        load.wait()
-        store.start()
-    for copy in stores:
+    for copy in copies:
         copy.wait()
 
 
@@ -454,7 +452,7 @@
             jax.ShapeDtypeStruct((1, 64, 1024), F32),
         ),
         in_specs=[any_space, pl.BlockSpec(memory_space=pltpu.SMEM), any_space, any_space, any_space],
-        out_specs=(any_space, any_space),
+        out_specs=(pl.BlockSpec(memory_space=pltpu.VMEM),) * 2,
         scratch_shapes=[
             pltpu.VMEM((16, 64, 1024), BF),
             pltpu.VMEM((64, 1024), F32),
@@ -483,8 +481,8 @@
             pltpu.VMEM((16, 4, 1024), BF),
             pltpu.VMEM((64, 1024), F32),
             dma((6,)),
-            dma((3, 4, 2)), dma((3, 4, 2)),
-            dma((3, 4, 2)), dma((3, 4, 2)),
+            dma((3, CHUNKS, 2)), dma((3, CHUNKS, 2)),
+            dma((3, CHUNKS, 2)), dma((3, CHUNKS, 2)),
             dma((2, 8)), dma((8, 2)),
             dma((4,)), dma((4,)), dma((4,)), dma((4,)),
             dma((8, 4)), dma((8, 4)), dma((8, 4)), dma((8, 4)),
@@ -493,7 +491,7 @@
             dma((16,)), dma((16,)),
         ],
         compiler_params=pltpu.CompilerParams(
-            collective_id=0, has_side_effects=True, vmem_limit_bytes=60 * 2**20
+            collective_id=0, has_side_effects=True, vmem_limit_bytes=54800 * 1024
         ),
     )(grad_partial, owner_slots, jnp.swapaxes(left_roots, 1, 2), right_roots, momentum)
     vmem = pl.BlockSpec(memory_space=pltpu.VMEM)
@@ -503,10 +501,10 @@
             jax.ShapeDtypeStruct((16, 4, 1024), BF),
             jax.ShapeDtypeStruct((1, 64, 1024), F32),
         ),
-        in_specs=[any_space, any_space],
+        in_specs=[vmem, vmem],
         out_specs=(any_space, any_space),
-        scratch_shapes=[dma((4,)), pltpu.VMEM((16, 4, 1024), BF), pltpu.VMEM((1, 64, 1024), F32)],
-        compiler_params=pltpu.CompilerParams(vmem_limit_bytes=60 * 2**20),
+        scratch_shapes=[dma((2,))],
+        compiler_params=pltpu.CompilerParams(vmem_limit_bytes=2 * 2**20),
     )(direction, new_momentum)
 
 

time: 71.1 us -> 69.5 us (0.977)
  Pallas kernels: 70.3 us -> 68.1 us
    pallas_call x1, Pallas kernels: 68.6 us -> 67.3 us  [body(): pl.pallas_call(kernel, out_shape=(jax.ShapeDtypeStruct((16, 4, 1024), BF)...]
    pallas_call x1, Pallas kernels: 1.73 us -> 0.76 us  [body(): pl.pallas_call(last, out_shape=(jax.ShapeDtypeStruct((16, 4, 1024), BF),...]
where the time goes in v3:
time: 69.5 us; the launch traced here: 69.4 us
  Pallas kernels  68.1 us (98%)
    pallas_call x1, Pallas kernels, body(): pl.pallas_call(kernel, out_shape=(jax.ShapeDtypeStruct((16, 4, 1024), BF)...  67.3 us

profile of v3, /device:TPU:1, one launch (start us, length us, event | category | flops | bytes accessed | tf_op | source)
XLA Modules:
  0.0 69.4 jit_solution(11071934015129082700)
XLA Ops:
  0.6 0.0 copy-start
  0.6 0.6 copy-done
  1.3 67.3 %shard_map.68 = (bf16[16,4,1024]{2,1,0:T(4,128)(2,1)S(1)}, f32[1,64,1024]{2,1,0:T(8,128)S(1)}) custom-call(bf16[1,16,64,1024]{3,2,1,0:T(8,128)(2,1)} %gp.1, s32[16]{0:T(128)S(1)} %copy-done, f32[1,64,1024]{2,1,0:T(8,128)} %bitcast.1, f32[1,64,1024]{2,1,0:T(8,128)} %rr.1, f32[1,64,1024]{2,1,0:T(8,128)} %mo.1), custom_call_target="tpu_custom_call" | custom-call | tf_op jit(solution)/shard_map/pallas_call | solution.py:448
  68.6 0.8 %shard_map.69 = (bf16[16,4,1024]{2,1,0:T(4,128)(2,1)}, f32[1,64,1024]{2,1,0:T(8,128)}) custom-call(bf16[16,4,1024]{2,1,0:T(4,128)(2,1)S(1)} %get-tuple-element.4.d_in, f32[1,64,1024]{2,1,0:T(8,128)S(1)} %get-tuple-element.5.m_in), custom_call_target="tpu_custom_call" | custom-call | tf_op jit(solution)/shard_map/pallas_call | solution.py:498
Async XLA Ops:
  0.6 0.7 copy-start

commit v4 on v3

--- a/solution.py
+++ b/solution.py
@@ -11,11 +11,12 @@
 MESH = pl.DeviceIdType.MESH
 BF = jnp.bfloat16
 F32 = jnp.float32
-PARTS = ((0, 2), (2, 2), (4, 2), (6, 2))
-CHUNKS = len(PARTS)
+PARTS = ((0, 2), (2, 2), (4, 1), (5, 3))
+EARLY = 5
+CHUNKS = len(PARTS) - 1
 OFFSETS = (4, 3, 5, 2, 6, 1, 7, 0)
-PASS1 = (True, True, True, True, True, True, False, False)
-PASS2 = (True, True, True, True, True, True, False, False)
+PASS1 = (True,) * 5 + (False,) * 3
+PASS2 = (True,) * 5 + (False,) * 3
 PASSR = True
 PASSL = True
 NT = (((1,), (1,)), ((), ()))
@@ -38,9 +39,9 @@
 
 def kernel(
     gp, own, lr, rr, mo, dir_o, nm_o,
-    gv, lv, rv, mv, stx, sty, r1x, r1y, s1x, s1y, r2x, r2y, zt, gbuf, hbuf, lg, rg,
+    gv, lv, rv, mv, stx, sty, r1x, r1y, s1x, s1y, r2x, r2y, ez, r1e, s1e, r2e, zt, gbuf, hbuf, lg, rg,
     pt, pr, scx, scy, h32, hb, fin, ob, nm,
-    loc, s1s, s1r, s2s, s2r, zs, zr, ls, lrc, rs, rrc, g1s, g1r, g2s, g2r, ts, tr,
+    loc, es, er, e1s, e1r, e2s, e2r, s1s, s1r, s2s, s2r, zs, zr, ls, lrc, rs, rrc, g1s, g1r, g2s, g2r, ts, tr,
     cxs, cxr, cys, cyr, fs, fr,
 ):
     dp = lax.axis_index("dp")
@@ -181,6 +182,79 @@
         else:
             pl.when(core == 0)(lambda: exchange(q, 1).wait_send())
             pl.when(core == 1)(lambda: exchange(q, 0).wait_send())
+
+    def early(q, target):
+        staged = (stx, sty)[target]
+        e = q - EARLY
+        device = {"shard": lax.rem(z + OFFSETS[q], 8) * 2 + target}
+        return remote(staged.at[:, q], ez.at[:, 2 * e + core], es.at[target, e], er.at[e, core], device)
+
+    def send_early(q):
+        if OFFSETS[q]:
+            early(q, 0).start()
+            early(q, 1).start()
+        else:
+            @pl.when(core == 0)
+            def _():
+                early(q, 1).start()
+                ez[:, 2 * (q - EARLY)] = stx[:, q]
+
+            @pl.when(core == 1)
+            def _():
+                early(q, 0).start()
+                ez[:, 2 * (q - EARLY) + 1] = sty[:, q]
+
+    def wait_early(q):
+        e = q - EARLY
+        for source in range(2):
+            def wait():
+                remote(stx.at[:, q], ez.at[:, 2 * e + source], es.at[0, e], er.at[e, source], {"shard": shard}).wait_recv()
+
+            if OFFSETS[q]:
+                wait()
+            else:
+                pl.when(core != source)(wait)
+
+    def sent_early(q):
+        if OFFSETS[q]:
+            early(q, 0).wait_send()
+            early(q, 1).wait_send()
+        else:
+            pl.when(core == 0)(lambda: early(q, 1).wait_send())
+            pl.when(core == 1)(lambda: early(q, 0).wait_send())
+
+    def early1(q):
+        e = q - EARLY
+        part = pl.ds(2 * e, 2)
+        return [
+            remote(ez.at[step(u, k), part], r1e.at[k - 1, part], e1s.at[k - 1, e], e1r.at[k - 1, e], to_u(k))
+            for k in range(1, 4)
+        ]
+
+    def early2(q):
+        e = q - EARLY
+        part = pl.ds(2 * e, 2)
+        return [
+            remote(s1e.at[step(v, k), part], r2e.at[k - 1, part], e2s.at[k - 1, e], e2r.at[k - 1, e], to_v(k))
+            for k in range(1, 4)
+        ]
+
+    def early_sum1(q):
+        for e in (2 * (q - EARLY), 2 * (q - EARLY) + 1):
+            total = ez[u, e].astype(F32)
+            for k in range(3):
+                total = total + r1e[k, e].astype(F32)
+            for j in range(4):
+                s1e[j, e] = total[:, 256 * j : 256 * j + 256]
+
+    def early_sum2(q):
+        for source in range(2):
+            e = 2 * (q - EARLY) + source
+            total = s1e[v, e]
+            for k in range(3):
+                total = total + r2e[k, e]
+            slot = 2 * lax.rem(z + 8 - OFFSETS[q], 8) + source
+            gbuf[slot, v, 0], gbuf[slot, v, 1] = split(total)
 
     def pair(q):
         return pl.ds(2 * lax.rem(z + 8 - OFFSETS[q], 8), 2)
@@ -275,6 +349,10 @@
         if c == 0:
             pl.semaphore_wait(barrier, 21)
         start_all(stage1(c))
+        if c == 0:
+            for q in slots(CHUNKS):
+                stage(q)
+                send_early(q)
 
     load_r.wait()
     rg[u, 0], rg[u, 1] = split(rv[...])
@@ -295,8 +373,23 @@
 
     def spread_rows(c):
         for q in slots(c):
-            wait_z(q)
+            if c < CHUNKS:
+                wait_z(q)
+            else:
+                recv_all(early2(q))
+                early_sum2(q)
             gather1(q).start()
+
+    def early_first():
+        for q in slots(CHUNKS):
+            wait_early(q)
+            start_all(early1(q))
+
+    def early_second():
+        for q in slots(CHUNKS):
+            recv_all(early1(q))
+            early_sum1(q)
+            start_all(early2(q))
 
     def pass_rows(c):
         for q in slots(c):
@@ -325,15 +418,15 @@
         scx[x, 0] = fold(tile * tile)
 
     sum_first(0)
+    early_first()
     sum_first(1)
     sum_first(2)
-    sum_first(3)
+    sum_second(0)
     rights.start()
-    sum_second(0)
+    sum_second(2)
     sum_second(1)
-    sum_second(2)
+    early_second()
     rights.go_on()
-    sum_second(3)
     lefts.start()
     spread_rows(0)
     spread_rows(1)
@@ -353,12 +446,12 @@
     pass_products(0)
     pass_products(1)
     pass_products(2)
-    pass_products(3)
     lefts.wait()
     multiply_left(0)
+    pass_products(3)
     multiply_left(1)
+    multiply_left(3)
     multiply_left(2)
-    multiply_left(3)
 
     tile = pt[...].reshape(256, 256)
     scx[x, 1] = fold(tile * tile)
@@ -377,8 +470,12 @@
     start_all(norms_y)
     for c in range(CHUNKS):
         send_all(stage2(c))
-    for q in range(8):
+    for q in range(EARLY):
         sent_z(q)
+    for q in slots(CHUNKS):
+        sent_early(q)
+        send_all(early1(q))
+        send_all(early2(q))
     recv_all(turn)
     recv_all(norms_y)
     sums = scy[0] + scy[1] + scy[2] + scy[3]
@@ -466,6 +563,10 @@
             pltpu.VMEM((4, 8, 16, 256), F32),
             pltpu.VMEM((3, 8, 16, 256), F32),
             pltpu.VMEM((3, 8, 16, 256), F32),
+            pltpu.VMEM((4, 6, 16, 1024), BF),
+            pltpu.VMEM((3, 6, 16, 1024), BF),
+            pltpu.VMEM((4, 6, 16, 256), F32),
+            pltpu.VMEM((3, 6, 16, 256), F32),
             pltpu.VMEM((2, 8, 2, 16, 256), BF),
             pltpu.VMEM((16, 4, 2, 16, 256), BF),
             pltpu.VMEM((2, 16, 4, 16, 256), BF),
@@ -481,6 +582,8 @@
             pltpu.VMEM((16, 4, 1024), BF),
             pltpu.VMEM((64, 1024), F32),
             dma((6,)),
+            dma((2, 3)), dma((3, 2)),
+            dma((3, 3)), dma((3, 3)), dma((3, 3)), dma((3, 3)),
             dma((3, CHUNKS, 2)), dma((3, CHUNKS, 2)),
             dma((3, CHUNKS, 2)), dma((3, CHUNKS, 2)),
             dma((2, 8)), dma((8, 2)),

time: 69.5 us -> 68.7 us (0.988)
  Pallas kernels: 68.1 us -> 67.3 us
    pallas_call x1, Pallas kernels: 67.3 us -> 66.5 us  [body(): pl.pallas_call(kernel, out_shape=(jax.ShapeDtypeStruct((16, 4, 1024), BF)...]
where the time goes in v4:
time: 68.7 us; the launch traced here: 68.6 us
  Pallas kernels  67.3 us (98%)
    pallas_call x1, Pallas kernels, body(): pl.pallas_call(kernel, out_shape=(jax.ShapeDtypeStruct((16, 4, 1024), BF)...  66.5 us

profile of v4, /device:TPU:1, one launch (start us, length us, event | category | flops | bytes accessed | tf_op | source)
XLA Modules:
  0.0 68.6 jit_solution(12113673704402127749)
XLA Ops:
  0.6 0.0 copy-start
  0.6 0.6 copy-done
  1.3 66.5 %shard_map.68 = (bf16[16,4,1024]{2,1,0:T(4,128)(2,1)S(1)}, f32[1,64,1024]{2,1,0:T(8,128)S(1)}) custom-call(bf16[1,16,64,1024]{3,2,1,0:T(8,128)(2,1)} %gp.1, s32[16]{0:T(128)S(1)} %copy-done, f32[1,64,1024]{2,1,0:T(8,128)} %bitcast.1, f32[1,64,1024]{2,1,0:T(8,128)} %rr.1, f32[1,64,1024]{2,1,0:T(8,128)} %mo.1), custom_call_target="tpu_custom_call" | custom-call | tf_op jit(solution)/shard_map/pallas_call | solution.py:545
  67.8 0.8 %shard_map.69 = (bf16[16,4,1024]{2,1,0:T(4,128)(2,1)}, f32[1,64,1024]{2,1,0:T(8,128)}) custom-call(bf16[16,4,1024]{2,1,0:T(4,128)(2,1)S(1)} %get-tuple-element.4.d_in, f32[1,64,1024]{2,1,0:T(8,128)S(1)} %get-tuple-element.5.m_in), custom_call_target="tpu_custom_call" | custom-call | tf_op jit(solution)/shard_map/pallas_call | solution.py:601
Async XLA Ops:
  0.6 0.7 copy-start

commit v5 on v4

--- a/solution.py
+++ b/solution.py
@@ -40,9 +40,9 @@
 def kernel(
     gp, own, lr, rr, mo, dir_o, nm_o,
     gv, lv, rv, mv, stx, sty, r1x, r1y, s1x, s1y, r2x, r2y, ez, r1e, s1e, r2e, zt, gbuf, hbuf, lg, rg,
-    pt, pr, scx, scy, h32, hb, fin, ob, nm,
-    loc, es, er, e1s, e1r, e2s, e2r, s1s, s1r, s2s, s2r, zs, zr, ls, lrc, rs, rrc, g1s, g1r, g2s, g2r, ts, tr,
-    cxs, cxr, cys, cyr, fs, fr,
+    pt, pr, scx, h32, hb, fin, ob, nm,
+    loc, known, es, er, e1s, e1r, e2s, e2r, s1s, s1r, s2s, s2r, zs, zr, ls, lrc, rs, rrc, g1s, g1r, g2s, g2r, ts, tr,
+    cxs, cxr, fs, fr,
 ):
     dp = lax.axis_index("dp")
     shard = lax.axis_index("shard")
@@ -59,6 +59,9 @@
 
     def to_y(k):
         return {"dp": step(y, k) * 4 + x}
+
+    def to_dp(k):
+        return {"dp": step(y, k // 4) * 4 + step(x, k % 4)}
 
     def to_u(k):
         return {"dp": (1 - core) * (y * 4 + step(x, k)) + core * (step(y, k) * 4 + x)}
@@ -93,13 +96,26 @@
     load_m.start()
 
     barrier = pltpu.get_barrier_semaphore()
-    for k in range(1, 4):
-        pl.semaphore_signal(barrier, inc=1, device_id=to_x(k), device_id_type=MESH)
-        pl.semaphore_signal(barrier, inc=1, device_id=to_y(k), device_id_type=MESH)
     for k in range(1, 16):
-        pl.semaphore_signal(
-            barrier, inc=1, device_id={"shard": lax.rem(shard + k, 16)}, device_id_type=MESH
-        )
+        pl.semaphore_signal(barrier, inc=1, device_id=to_dp(k), device_id_type=MESH)
+
+    def along_z(k):
+        return {"shard": lax.rem(z + k + 8, 8) * 2 + core}
+
+    other_core = {"shard": z * 2 + 1 - core}
+    cross = ({"shard": lax.rem(z + 1, 8) * 2 + 1 - core}, {"shard": lax.rem(z + 7, 8) * 2 + 1 - core})
+    near = (along_z(1), along_z(-1), other_core)
+    for device in near + cross:
+        pl.semaphore_signal(barrier, inc=1, device_id=device, device_id_type=MESH)
+
+    rounds = (near, (along_z(2), along_z(-2)), (other_core,))
+
+    def tell(i):
+        for device in rounds[i]:
+            pl.semaphore_signal(known.at[i], inc=1, device_id=device, device_id_type=MESH)
+
+    def hear(i):
+        pl.semaphore_wait(known.at[i], len(rounds[i]))
 
     def block_of(slot):
         found = jnp.int32(0)
@@ -347,9 +363,10 @@
         for q in slots(c):
             stage(q)
         if c == 0:
-            pl.semaphore_wait(barrier, 21)
+            pl.semaphore_wait(barrier, 20)
         start_all(stage1(c))
         if c == 0:
+            tell(0)
             for q in slots(CHUNKS):
                 stage(q)
                 send_early(q)
@@ -412,15 +429,28 @@
         product = left_times(slots(c)).reshape(4, 64, 256)
         pt[...] = product if c == 0 else pt[...] + product
 
+    def norms(kind):
+        part = scx.at[kind, dp]
+        return [
+            remote(part, part, cxs.at[kind, k], cxr.at[kind, k], to_dp(k))
+            for k in (10, 6, 14, 9, 11, 5, 7, 13, 15, 2, 8, 1, 3, 4, 12)
+        ]
+
     def norm_of_gradient():
         tile = gbuf[:, v]
         tile = (tile[:, 0].astype(F32) + tile[:, 1].astype(F32)).reshape(256, 256)
-        scx[x, 0] = fold(tile * tile)
+        scx[0, dp] = fold(tile * tile)
+        start_all(norms(0))
 
     sum_first(0)
+    hear(0)
+    tell(1)
     early_first()
+    hear(1)
+    tell(2)
     sum_first(1)
     sum_first(2)
+    hear(2)
     sum_second(0)
     rights.start()
     sum_second(2)
@@ -454,20 +484,15 @@
     multiply_left(2)
 
     tile = pt[...].reshape(256, 256)
-    scx[x, 1] = fold(tile * tile)
-
-    norms_x = [remote(scx.at[x], scx.at[x], cxs.at[k - 1], cxr.at[k - 1], to_x(k)) for k in range(1, 4)]
-    norms_y = [remote(scy.at[y], scy.at[y], cys.at[k - 1], cyr.at[k - 1], to_y(k)) for k in range(1, 4)]
+    scx[1, dp] = fold(tile * tile)
+
     turn = [remote(pt.at[step(v, k)], pr.at[v], ts.at[k - 1], tr.at[k - 1], to_v(k)) for k in range(1, 4)]
-    start_all(norms_x)
+    start_all(norms(1))
     start_all(turn)
     pr[v] = pt[v]
     load_m.wait()
     for c in range(CHUNKS):
         send_all(stage1(c))
-    recv_all(norms_x)
-    scy[y] = scx[0] + scx[1] + scx[2] + scx[3]
-    start_all(norms_y)
     for c in range(CHUNKS):
         send_all(stage2(c))
     for q in range(EARLY):
@@ -477,11 +502,11 @@
         send_all(early1(q))
         send_all(early2(q))
     recv_all(turn)
-    recv_all(norms_y)
-    sums = scy[0] + scy[1] + scy[2] + scy[3]
+    recv_all(norms(0))
+    recv_all(norms(1))
     entries = 1024 * 1024
-    grad_total = jnp.sum(sums[0], keepdims=True)
-    prec_total = jnp.sum(sums[1], keepdims=True)
+    grad_total = jnp.sum(scx[0].sum(axis=0), keepdims=True)
+    prec_total = jnp.sum(scx[1].sum(axis=0), keepdims=True)
     scale = jnp.sqrt(grad_total / entries + epsilon) / jnp.sqrt(prec_total / entries + epsilon)
 
     def update(columns):
@@ -515,8 +540,8 @@
     for k in order:
         back(k).start()
     fin[shard] = hb[shard]
-    send_all(norms_x)
-    send_all(norms_y)
+    send_all(norms(0))
+    send_all(norms(1))
     send_all(turn)
     rights.sent()
     lefts.sent()
@@ -574,14 +599,14 @@
             pltpu.VMEM((4, 2, 64, 1024), BF),
             pltpu.VMEM((4, 64, 256), F32),
             pltpu.VMEM((4, 64, 256), F32),
-            pltpu.VMEM((4, 2, 8, 128), F32),
-            pltpu.VMEM((4, 2, 8, 128), F32),
+            pltpu.VMEM((2, 16, 8, 128), F32),
             pltpu.VMEM((64, 1024), F32),
             pltpu.VMEM((16, 4, 1024), BF),
             pltpu.VMEM((16, 4, 1024), BF),
             pltpu.VMEM((16, 4, 1024), BF),
             pltpu.VMEM((64, 1024), F32),
             dma((6,)),
+            pltpu.SemaphoreType.REGULAR((3,)),
             dma((2, 3)), dma((3, 2)),
             dma((3, 3)), dma((3, 3)), dma((3, 3)), dma((3, 3)),
             dma((3, CHUNKS, 2)), dma((3, CHUNKS, 2)),
@@ -590,7 +615,7 @@
             dma((4,)), dma((4,)), dma((4,)), dma((4,)),
             dma((8, 4)), dma((8, 4)), dma((8, 4)), dma((8, 4)),
             dma((3,)), dma((3,)),
-            dma((3,)), dma((3,)), dma((3,)), dma((3,)),
+            dma((2, 16)), dma((2, 16)),
             dma((16,)), dma((16,)),
         ],
         compiler_params=pltpu.CompilerParams(

time: 68.7 us -> 67.6 us (0.984)
  Pallas kernels: 67.3 us -> 66.2 us
    pallas_call x1, Pallas kernels: 66.5 us -> 65.4 us  [body(): pl.pallas_call(kernel, out_shape=(jax.ShapeDtypeStruct((16, 4, 1024), BF)...]
where the time goes in v5:
time: 67.6 us; the launch traced here: 67.5 us
  Pallas kernels  66.2 us (98%)
    pallas_call x1, Pallas kernels, body(): pl.pallas_call(kernel, out_shape=(jax.ShapeDtypeStruct((16, 4, 1024), BF)...  65.4 us

profile of v5, /device:TPU:1, one launch (start us, length us, event | category | flops | bytes accessed | tf_op | source)
XLA Modules:
  0.0 67.5 jit_solution(2815094147489336617)
XLA Ops:
  0.6 0.0 copy-start
  0.6 0.6 copy-done
  1.3 65.4 %shard_map.68 = (bf16[16,4,1024]{2,1,0:T(4,128)(2,1)S(1)}, f32[1,64,1024]{2,1,0:T(8,128)S(1)}) custom-call(bf16[1,16,64,1024]{3,2,1,0:T(8,128)(2,1)} %gp.1, s32[16]{0:T(128)S(1)} %copy-done, f32[1,64,1024]{2,1,0:T(8,128)} %bitcast.1, f32[1,64,1024]{2,1,0:T(8,128)} %rr.1, f32[1,64,1024]{2,1,0:T(8,128)} %mo.1), custom_call_target="tpu_custom_call" | custom-call | tf_op jit(solution)/shard_map/pallas_call | solution.py:570
  66.7 0.8 %shard_map.69 = (bf16[16,4,1024]{2,1,0:T(4,128)(2,1)}, f32[1,64,1024]{2,1,0:T(8,128)}) custom-call(bf16[16,4,1024]{2,1,0:T(4,128)(2,1)S(1)} %get-tuple-element.4.d_in, f32[1,64,1024]{2,1,0:T(8,128)S(1)} %get-tuple-element.5.m_in), custom_call_target="tpu_custom_call" | custom-call | tf_op jit(solution)/shard_map/pallas_call | solution.py:626
Async XLA Ops:
  0.6 0.7 copy-start

commit v6 on v5

--- a/solution.py
+++ b/solution.py
@@ -451,8 +451,8 @@
     sum_first(1)
     sum_first(2)
     hear(2)
+    rights.start()
     sum_second(0)
-    rights.start()
     sum_second(2)
     sum_second(1)
     early_second()

time: 67.6 us -> 67.6 us (level)
  no operation moved by 1% of the time
where the time goes in v6:
time: 67.6 us; the launch traced here: 67.5 us
  Pallas kernels  66.2 us (98%)
    pallas_call x1, Pallas kernels, body(): pl.pallas_call(kernel, out_shape=(jax.ShapeDtypeStruct((16, 4, 1024), BF)...  65.4 us

profile of v6, /device:TPU:1, one launch (start us, length us, event | category | flops | bytes accessed | tf_op | source)
XLA Modules:
  0.0 67.5 jit_solution(6610082978562412146)
XLA Ops:
  0.6 0.0 copy-start
  0.6 0.6 copy-done
  1.3 65.4 %shard_map.68 = (bf16[16,4,1024]{2,1,0:T(4,128)(2,1)S(1)}, f32[1,64,1024]{2,1,0:T(8,128)S(1)}) custom-call(bf16[1,16,64,1024]{3,2,1,0:T(8,128)(2,1)} %gp.1, s32[16]{0:T(128)S(1)} %copy-done, f32[1,64,1024]{2,1,0:T(8,128)} %bitcast.1, f32[1,64,1024]{2,1,0:T(8,128)} %rr.1, f32[1,64,1024]{2,1,0:T(8,128)} %mo.1), custom_call_target="tpu_custom_call" | custom-call | tf_op jit(solution)/shard_map/pallas_call | solution.py:570
  66.7 0.8 %shard_map.69 = (bf16[16,4,1024]{2,1,0:T(4,128)(2,1)}, f32[1,64,1024]{2,1,0:T(8,128)}) custom-call(bf16[16,4,1024]{2,1,0:T(4,128)(2,1)S(1)} %get-tuple-element.4.d_in, f32[1,64,1024]{2,1,0:T(8,128)S(1)} %get-tuple-element.5.m_in), custom_call_target="tpu_custom_call" | custom-call | tf_op jit(solution)/shard_map/pallas_call | solution.py:626
Async XLA Ops:
  0.6 0.7 copy-start
